TPU v7x, 32 devices: a whole 2x2x4 slice. The times are simulated.
32 devices in a mesh: groups: 2 (over y), neuron: 8 (over z, x), expert: 2 (over core).
Axes of the slice: x: 2, y: 2, z: 4, core: 2. Of those that a mesh axis runs over, the one named last changes fastest.
Arguments:
- tokens: bfloat16 [128, 4096], P(('groups', 'neuron', 'expert')), parts along dimension 0, may hold values from -6 to 6
- routes: int32 [128, 2], P(('groups', 'neuron', 'expert')), parts along dimension 0, may hold values from 0 to 7, as said below
- route_weights: int32 [128, 2], P(('groups', 'neuron', 'expert')), parts along dimension 0, may hold values from 6554 to 65535
- block_masks: int32 [128, 2, 4], P(('groups', 'neuron', 'expert')), parts along dimension 0, may hold values from 0 to 1073741823, as said below
- block_list: int32 [4, 120], P(('groups', 'expert')), parts along dimension 0, may hold values from 0 to 111, as said below
- gate_rows: bfloat16 [4, 15360, 4096], P(('groups', 'expert'), 'neuron'), parts along dimension 0, as said below
- up_rows: bfloat16 [4, 15360, 4096], P(('groups', 'expert'), 'neuron'), parts along dimension 0, as said below
- down_rows: bfloat16 [4, 15360, 4096], P(('groups', 'expert'), 'neuron'), parts along dimension 0, as said below
Outputs:
- moe_output: bfloat16 [128, 4096], P(('groups', 'neuron', 'expert')), parts along dimension 0
There are 2 independent parts, one for each index of `groups`. A program takes and returns all parts, laid end to end along the dimension named above; each array names one. Nothing has to cross between parts.
Inputs may be any that keep to these rules, and one draw needn't show every extreme that they name: `routes`: each row names 2 different experts; in each aligned block of 8 rows every expert is named by exactly 2 rows. Bit i of word w of block_masks[t, r] marks row block 30 w + i of expert routes[t, r] as active; bits from 112 on are zero. A block that block_list places in two slots is active in every row that routes to its expert; any other block is active in exactly 1 of the 2 rows of an aligned block of 8 rows that route to its expert. `block_list`: slots are numbered along the neuron axis, 15 to a shard; every block of an expert sits in one slot, and 8 of them in two. `gate_rows`: the rows of slot s of expert e hold the block named by block_list[e, s]; two slots of one block hold equal rows. `up_rows`: as gate_rows. `down_rows`: as gate_rows.
All inputs are finite; a program needn't handle non-finite values.
Results may differ from a plain program's by a relative error of at most 0.005.
Values may be sent and summed in bfloat16 or wider, within the bound.
A program may use at most 128 MiB of HBM per device.

v0:
```python
import jax
import jax.numpy as jnp
from jax import lax
from jax.sharding import PartitionSpec as P

EXPERTS = 8


def mask_bits(mask_words, block_ids):
    shifted = jnp.right_shift(jnp.take(mask_words, block_ids // 30, axis=-1), block_ids % 30)
    return jnp.bitwise_and(shifted, 1)


def slot_copies(placing):
    slot_count = placing.shape[0]
    slot_order = jnp.arange(slot_count)
    matching = placing[:, None] == placing[None, :]
    earlier = jnp.sum(matching & (slot_order[None, :] < slot_order[:, None]), axis=1)
    doubled = (jnp.sum(matching, axis=1) > 1).astype(jnp.int32)
    return (earlier, doubled)


def choose_rows(active, earlier, routed):
    position = jnp.arange(routed)
    taking = active * (earlier == 0).astype(jnp.int32)
    target = jnp.broadcast_to(position, taking.shape)
    slot_ids = jnp.arange(routed)
    return (taking[..., None, :] == 1) & (target[..., None, :] == slot_ids[:, None])


def block_outputs(arrived, gate_local, up_local, down_local):
    gate_pre = jnp.einsum("nskd,sud->nsku", arrived, gate_local, preferred_element_type=jnp.float32)
    up_pre = jnp.einsum("nskd,sud->nsku", arrived, up_local, preferred_element_type=jnp.float32)
    hidden = (jnp.maximum(gate_pre, 0.0) * jnp.maximum(up_pre, 0.0)).astype(jnp.bfloat16)
    return jnp.einsum("nsku,sud->nskd", hidden, down_local, preferred_element_type=jnp.float32)


def local(tokens, routes, route_weights, block_masks, block_list, gate_rows, up_rows, down_rows):
    pair_tokens, pair_routes, pair_weights, pair_masks = (
        lax.all_gather(tokens, "expert", axis=0, tiled=True),
        lax.all_gather(routes, "expert", axis=0, tiled=True),
        lax.all_gather(route_weights, "expert", axis=0, tiled=True),
        lax.all_gather(block_masks, "expert", axis=0, tiled=True),
    )
    expert = lax.axis_index("expert")
    neurons = lax.axis_size("neuron")
    row_count = pair_tokens.shape[0]
    width = pair_tokens.shape[1]
    routed = 2 * row_count // EXPERTS
    is_named = (pair_routes == expert).astype(jnp.int32)
    chosen = jnp.sum(is_named, axis=1)
    scaled = jnp.sum(is_named * pair_weights, axis=1).astype(jnp.float32) / 65536.0
    mask_words = jnp.sum(is_named[:, :, None] * pair_masks, axis=1)
    route_rank = jnp.cumsum(chosen) - chosen
    picking = (route_rank[None, :] == jnp.arange(routed)[:, None]) & (chosen[None, :] == 1)
    picked_tokens = jnp.dot(
        picking.astype(jnp.bfloat16), pair_tokens, preferred_element_type=jnp.float32
    ).astype(jnp.bfloat16)
    picked_words = jnp.sum(picking.astype(jnp.int32)[:, :, None] * mask_words[None, :, :], axis=1)
    picked_scale = jnp.sum(picking.astype(jnp.float32) * scaled[None, :], axis=1)
    placing = block_list[0]
    slot_count = placing.shape[0]
    slot_dev = slot_count // neurons
    earlier, doubled = slot_copies(placing)
    active = jnp.swapaxes(mask_bits(picked_words, placing), 0, 1)
    selection = choose_rows(active, earlier[:, None], routed)
    capacity = selection.shape[1]
    gate_local = gate_rows[0].reshape(slot_dev, -1, width)
    up_local = up_rows[0].reshape(slot_dev, -1, width)
    down_local = down_rows[0].reshape(slot_dev, -1, width)
    outgoing = jnp.einsum(
        "scr,rd->scd",
        selection.astype(jnp.bfloat16),
        picked_tokens,
        preferred_element_type=jnp.float32,
    ).astype(jnp.bfloat16)
    outgoing = outgoing.reshape(neurons, slot_dev, capacity, width)
    returned = lax.all_to_all(
        block_outputs(
            lax.all_to_all(outgoing, "neuron", split_axis=0, concat_axis=0, tiled=True),
            gate_local,
            up_local,
            down_local,
        ),
        "neuron",
        split_axis=0,
        concat_axis=0,
        tiled=True,
    )
    returned = returned.reshape(slot_count, capacity, width)
    summed = jnp.einsum(
        "scr,scd->rd", selection.astype(jnp.float32), returned, precision=lax.Precision.HIGHEST
    )
    weighted = summed * picked_scale[:, None]
    spread_back = jnp.einsum(
        "rg,rd->gd", picking.astype(jnp.float32), weighted, precision=lax.Precision.HIGHEST
    )
    own_rows = lax.psum_scatter(spread_back, "expert", scatter_dimension=0, tiled=True)
    return own_rows.astype(jnp.bfloat16)


def solution(mesh):
    placed = (
        P(("groups", "neuron", "expert"), None),
        P(("groups", "neuron", "expert"), None),
        P(("groups", "neuron", "expert"), None),
        P(("groups", "neuron", "expert"), None, None),
        P(("groups", "expert"), None),
        P(("groups", "expert"), "neuron", None),
        P(("groups", "expert"), "neuron", None),
        P(("groups", "expert"), "neuron", None),
    )
    return jax.shard_map(
        local,
        mesh=mesh,
        in_specs=placed,
        out_specs=P(("groups", "neuron", "expert"), None),
        check_vma=False,
    )
```

profile of v0, /device:TPU:0, one launch (start us, length us, event | category | flops | bytes accessed | tf_op | source)
XLA Modules:
  0.0 197.5 jit_solution(12250197118132065469)
XLA Ops:
  0.0 2.1 %all-gather = s32[2,4,2]{1,2,0:T(2,128)S(1)} all-gather(s32[1,4,2]{1,2,0:T(2,128)} %bitcast.64), channel_id=1, replica_groups=mesh['groups'=2,'neuron'=8,'expert'=2] {'expert'}, dimensions={0}, use_global_device_ids=true | all-gather | bytes 96 | tf_op jit(solution)/shard_map/all_gather | solution.py:41
  2.1 2.0 %all-gather.2 = s32[2,4,2]{1,2,0:T(2,128)S(1)} all-gather(s32[1,4,2]{1,2,0:T(2,128)} %bitcast.65), channel_id=1, replica_groups=mesh['groups'=2,'neuron'=8,'expert'=2] {'expert'}, dimensions={0}, use_global_device_ids=true | all-gather | bytes 96 | tf_op jit(solution)/shard_map/all_gather | solution.py:42
  4.1 0.1 reshape.180
  4.3 0.7 fusion.26
  5.0 0.7 fusion.25
  5.6 0.2 reduce-window.8
  5.8 0.1 reshape.184
  5.9 0.1 select_reduce_fusion.1
  6.0 0.1 copy.64
  6.1 1.9 all_gather.13
  8.1 0.1 multiply_reduce_fusion
  8.2 0.1 copy.53
  8.3 0.1 multiply_reduce_fusion.1
  8.4 0.1 copy.54
  8.5 0.6 gather_fusion
  9.2 0.9 convert_reduce_fusion
  10.1 0.7 compare_convert_fusion
  10.8 2.1 %all-gather.1 = bf16[2,4,4096]{2,1,0:T(4,128)(2,1)S(1)} all-gather(bf16[1,4,4096]{2,1,0:T(4,128)(2,1)} %bitcast.62), channel_id=1, replica_groups=mesh['groups'=2,'neuron'=8,'expert'=2] {'expert'}, dimensions={0}, use_global_device_ids=true | all-gather | bytes 98304 | tf_op jit(solution)/shard_map/all_gather | solution.py:40
  12.9 0.8 convolution_convert_fusion
  13.7 2.1 %copy.56 = bf16[120,2,4096]{2,1,0:T(2,128)(2,1)S(1)} copy(bf16[120,2,4096]{2,0,1:T(8,128)(2,1)S(1)} %convolution_convert_fusion) | data formatting | bytes 3932160 | tf_op jit(solution)/shard_map/convert_element_type | solution.py:76
  15.8 53.0 %all_to_all.10 = bf16[8,15,2,4096]{3,2,1,0:T(2,128)(2,1)S(1)} all-to-all(bf16[8,15,2,4096]{3,2,1,0:T(2,128)(2,1)S(1)} %bitcast.61), channel_id=1, replica_groups=mesh['groups'=2,'neuron'=8,'expert'=2] {'neuron'}, dimensions={0} | all-to-all | bytes 3932160 | tf_op jit(solution)/shard_map/all_to_all | solution.py:80
  68.8 7.7 %fusion.13 = f32[15,8,2,128]{3,1,2,0:T(8,128)S(1)} fusion(bf16[15,128,4096,1]{2,1,3,0:T(8,128)(2,1)} %bitcast.59, bf16[8,15,2,4096]{3,2,1,0:T(2,128)(2,1)S(1)} %all_to_all.10), kind=kOutput, calls=%fused_computation.14 | convolution fusion | flops 251688960 | bytes 17817600 | tf_op jit(solution)/shard_map/nskd,sud->nsku/dot_general | solution.py:33
  76.5 7.7 %fusion.19 = bf16[8,15,2,128]{3,0,2,1:T(8,128)(2,1)S(1)} fusion(f32[15,8,2,128]{3,1,2,0:T(8,128)S(1)} %fusion.13, bf16[15,128,4096,1]{2,1,3,0:T(8,128)(2,1)} %bitcast.60, bf16[8,15,2,4096]{3,2,1,0:T(2,128)(2,1)S(1)} %all_to_all.10), kind=kOutput, calls=%fused_computation.16 | convolution fusion | flops 251750400 | bytes 17879040 | tf_op jit(solution)/shard_map/nskd,sud->nsku/dot_general | solution.py:32
  84.3 6.6 %convolution_bitcast_fusion = f32[8,15,2,4096]{3,0,2,1:T(8,128)S(1)} fusion(bf16[8,15,2,128]{3,0,2,1:T(8,128)(2,1)S(1)} %fusion.19, bf16[15,128,4096,1]{2,1,3,0:T(8,128)(2,1)} %bitcast.58), kind=kOutput, calls=%fused_computation.1 | convolution fusion | flops 251658240 | bytes 19722240 | tf_op jit(solution)/shard_map/nsku,sud->nskd/dot_general | solution.py:35
  90.9 4.9 %copy.59 = f32[8,15,2,4096]{3,2,1,0:T(2,128)} copy(f32[8,15,2,4096]{3,0,2,1:T(8,128)S(1)} %convolution_bitcast_fusion) | data formatting | bytes 7864320 | tf_op jit(solution)/shard_map/nsku,sud->nskd/transpose | solution.py:35
  95.9 4.9 %all-to-all-start.1 = ((f32[8,15,2,4096]{3,2,1,0:T(2,128)}), f32[8,15,2,4096]{3,2,1,0:T(2,128)}, u32[]{:S(2)}, u32[]{:S(2)}) async-start(f32[8,15,2,4096]{3,2,1,0:T(2,128)} %copy.59), calls=%async_computation.1 | async-start | bytes 7864320 | tf_op jit(solution)/shard_map/all_to_all | solution.py:78
  100.7 0.6 dynamic-slice
  102.0 85.2 %all-to-all-done.1 = f32[8,15,2,4096]{3,2,1,0:T(2,128)} async-done(((f32[8,15,2,4096]{3,2,1,0:T(2,128)}), f32[8,15,2,4096]{3,2,1,0:T(2,128)}, u32[]{:S(2)}, u32[]{:S(2)}) %all-to-all-start.1) | async-done | bytes 3932192 | tf_op jit(solution)/shard_map/all_to_all | solution.py:78
  187.2 5.5 %fusion = f32[2,4096]{1,0:T(2,128)S(1)} fusion(f32[120,2,4096]{2,1,0:T(2,128)} %bitcast.22, f32[2]{0:T(128)S(1)} %get-tuple-element.7, pred[120,2]{0,1:T(4,128)(4,1)S(1)} %multiply_compare_fusion), kind=kOutput, calls=%fused_computation.4 | convolution fusion | flops 23602112 | bytes 3965176 | tf_op jit(solution)/shard_map/scr,scd->rd/dot_general | solution.py:91
  192.7 0.3 fusion.28
  193.0 3.8 %all-reduce.2 = bf16[8,4096]{1,0:T(8,128)(2,1)S(1)} all-reduce(f32[8,4096]{1,0:T(8,128)S(1)} %fusion.28), channel_id=2, replica_groups=mesh['groups'=2,'neuron'=8,'expert'=2] {'expert'}, use_global_device_ids=true, to_apply=%region_7.8.clone | all-reduce | flops 32768 | bytes 196608
  196.8 0.6 dynamic-slice_convert_fusion
  (13 shorter events, 0.2 us)
Async XLA Ops:
  95.9 4.9 %copy-start = (u32[32]{0:T(128)S(1)}, u32[32]{0:T(128)}, u32[]{:S(2)}) copy-start(u32[32]{0:T(128)} %constant.65) | copy-start | bytes 388
  95.9 91.3 %all-to-all-start.1 = ((f32[8,15,2,4096]{3,2,1,0:T(2,128)}), f32[8,15,2,4096]{3,2,1,0:T(2,128)}, u32[]{:S(2)}, u32[]{:S(2)}) async-start(f32[8,15,2,4096]{3,2,1,0:T(2,128)} %copy.59), calls=%async_computation.1 | async-start | bytes 7864320 | tf_op jit(solution)/shard_map/all_to_all | solution.py:78
where the time goes:
time: 198 us; the launch traced here: 197 us
  waiting for transfers between devices  85.2 us (43%)
  blocking collectives  65 us (33%)
  matrix products  28.6 us (14%)
  local copies, waits for them, and re-layouts  9.47 us (5%)
  starting transfers between devices  4.86 us (2%)
  other arithmetic  3.55 us (2%)
    all_to_all x1, waiting for transfers between devices, local(): lax.all_to_all(block_outputs(lax.all_to_all(outgoing, 'neuron', split_axi...  85.2 us
    all_to_all x1, blocking collectives, local(): lax.all_to_all(outgoing, 'neuron', split_axis=0, concat_axis=0, tiled=True)  53 us
    dot_general x1, matrix products, block_outputs(): jnp.einsum('nskd,sud->nsku', arrived, gate_local, preferred_element_type=...  7.74 us
    dot_general x1, matrix products, block_outputs(): jnp.einsum('nskd,sud->nsku', arrived, up_local, preferred_element_type=jn...  7.74 us
    dot_general x1, matrix products, block_outputs(): jnp.einsum('nsku,sud->nskd', hidden, down_local, preferred_element_type=j...  6.62 us
    dot_general x1, matrix products, local(): jnp.einsum('scr,scd->rd', selection.astype(jnp.float32), returned, precis...  5.52 us
    transpose x1, local copies, waits for them, and re-layouts, block_outputs(): jnp.einsum('nsku,sud->nskd', hidden, down_local, preferred_element_type=j...  4.93 us
    all_to_all x1, starting transfers between devices, local(): lax.all_to_all(block_outputs(lax.all_to_all(outgoing, 'neuron', split_axi...  4.86 us
  transfers between devices with their start and end apart: 1, of which 1 were waited for; matrix products, arithmetic and copies ran while one was open for 0% of the time, Pallas kernels for 0%

commit v1 on v0

v1 whole, which is shorter than its diff:
```python
import functools

import jax
import jax.numpy as jnp
from jax import lax
from jax.experimental import pallas as pl
from jax.experimental.pallas import tpu as pltpu
from jax.sharding import PartitionSpec as P

BLK = 128
LANES = 128
UNITS = 4
F32 = jnp.float32
BF16 = jnp.bfloat16
MESH = pl.DeviceIdType.MESH


def total(value, axis):
    return jnp.sum(value, axis=axis, keepdims=True)


def picks_of(expert, routes, per_dev):
    low, high = None, None
    for half in range(2):
        named = jnp.max((routes[half] == expert).astype(F32), axis=1, keepdims=True)
        place = lax.broadcasted_iota(jnp.int32, (per_dev, 1), 0).astype(F32) + float(half * per_dev)
        least = jnp.min(jnp.where(named > 0.5, place, 1e6), axis=0, keepdims=True)
        most = jnp.max(jnp.where(named > 0.5, place, -1.0), axis=0, keepdims=True)
        low = least if low is None else jnp.minimum(low, least)
        high = most if high is None else jnp.maximum(high, most)
    return low, high


def kernel(
    neurons, chunk_slots,
    tok_in, routes_in, weights_in, masks_in, list_in, gate_hbm, up_hbm, down_hbm,
    out_ref,
    gate_v, up_v, down_v, pair_tok, pair_routes, pair_weights, pair_masks, slabs, lhs, bits_s,
    act, hid, acc, snd, rcv, rows_own, rows_other,
    gate_sem, up_sem, down_sem, pair_send, pair_recv, tok_send, tok_recv,
    out_send, out_recv, fin_send, fin_recv,
):
    me = lax.axis_index("neuron")
    expert = lax.axis_index("expert")
    other = 1 - expert
    per_dev, width = tok_in.shape
    subs = width // LANES
    unit = width // UNITS
    usubs = unit // LANES
    slots = gate_v.shape[0] // BLK
    rows = 2 * neurons
    chunk = chunk_slots * BLK
    chunks = slots // chunk_slots
    slab_rows = 2 * subs

    def weight_copy(hbm, vmem, sems, index):
        here = pl.ds(pl.multiple_of(index * chunk, chunk), chunk)
        return pltpu.make_async_copy(hbm.at[0, here, :], vmem.at[here, :], sems.at[index])

    def down_copy(index):
        return pltpu.make_async_copy(
            down_hbm.at[0, :, pl.ds(index * unit, unit)], down_v.at[index], down_sem.at[index]
        )

    for index in range(chunks):
        weight_copy(gate_hbm, gate_v, gate_sem, index).start()
        weight_copy(up_hbm, up_v, up_sem, index).start()
    for index in range(UNITS):
        down_copy(index).start()

    barrier = pltpu.get_barrier_semaphore()

    def greet(step, carry):
        pl.semaphore_signal(
            barrier, inc=1, device_id={"neuron": lax.rem(me + step, neurons)}, device_id_type=MESH
        )
        return carry

    pl.semaphore_signal(barrier, inc=1, device_id={"expert": other}, device_id_type=MESH)
    lax.fori_loop(1, neurons, greet, 0)

    pair_tok[expert] = tok_in[...].astype(F32).reshape(per_dev, subs, LANES).astype(BF16)
    pair_routes[expert] = routes_in[...]
    pair_weights[expert] = weights_in[...]
    pair_masks[expert] = masks_in[...]

    pl.semaphore_wait(barrier, neurons)

    def pair_copy(buffer, index):
        return pltpu.make_async_remote_copy(
            src_ref=buffer.at[expert], dst_ref=buffer.at[expert],
            send_sem=pair_send.at[index], recv_sem=pair_recv.at[index],
            device_id={"expert": other}, device_id_type=MESH,
        )

    pair_buffers = (pair_tok, pair_routes, pair_weights, pair_masks)
    for index, buffer in enumerate(pair_buffers):
        pair_copy(buffer, index).start()

    listed = list_in[...]
    slot_count = listed.shape[1]
    block_id = lax.broadcasted_iota(jnp.int32, (LANES, slot_count), 0)
    slot_id = lax.broadcasted_iota(jnp.int32, (LANES, slot_count), 1).astype(F32)
    first_slot = jnp.min(jnp.where(listed == block_id, slot_id, 1e6), axis=1, keepdims=True)
    own_slot = (lax.broadcasted_iota(jnp.int32, (LANES, LANES), 1) + me * slots).astype(F32)
    slot_lane = lax.broadcasted_iota(jnp.int32, (LANES, LANES), 1)
    holds = ((own_slot == first_slot) & (slot_lane < slots)).astype(F32).astype(BF16)

    for index, buffer in enumerate(pair_buffers):
        pair_copy(buffer, index).wait()

    routes = [pair_routes[half] for half in range(2)]
    picks = picks_of(expert, routes, per_dev)
    picks_other = picks_of(other, routes, per_dev)
    lane = lax.broadcasted_iota(jnp.int32, (1, LANES), 1)
    word_of = sum((lane >= 30 * word).astype(jnp.int32) for word in (1, 2, 3))
    shift = jnp.minimum(lane - 30 * word_of, 30)
    scales, bit_rows = [], []
    for pick in picks:
        scale, words = None, None
        for half in range(2):
            place = lax.broadcasted_iota(jnp.int32, (per_dev, 1), 0).astype(F32) + float(half * per_dev)
            for route in range(2):
                is_it = (routes[half][:, route:route + 1] == expert) & (place == pick)
                weight = total(jnp.where(is_it, pair_weights[half][:, route:route + 1].astype(F32), 0.0), 0)
                word = total(jnp.where(is_it, pair_masks[half, :, route, :], 0), 0)
                scale = weight if scale is None else scale + weight
                words = word if words is None else words + word
        scales.append(scale / 65536.0)
        spread = jnp.where(
            word_of == 0, words[:, 0:1],
            jnp.where(word_of == 1, words[:, 1:2], jnp.where(word_of == 2, words[:, 2:3], words[:, 3:4])),
        )
        bit_rows.append(jnp.bitwise_and(jnp.right_shift(spread, shift), 1).astype(F32))

    for row, pick in enumerate(picks):
        chosen = jnp.zeros((subs, LANES), F32)
        for token in range(2 * per_dev):
            gain = (pick == float(token)).astype(F32)
            chosen = chosen + gain * pair_tok[token // per_dev, token % per_dev].astype(F32)
        slabs[me, row * subs:(row + 1) * subs, :] = chosen.astype(BF16)
    line = lax.broadcasted_iota(jnp.int32, (16, LANES), 0)
    slabs[me, slab_rows:slab_rows + 16, :] = jnp.where(
        line == 0, bit_rows[0], jnp.where(line == 1, bit_rows[1], 0.0)
    ).astype(BF16)

    def token_copy(step, source):
        return pltpu.make_async_remote_copy(
            src_ref=slabs.at[source], dst_ref=slabs.at[source],
            send_sem=tok_send.at[step], recv_sem=tok_recv.at[source],
            device_id={"neuron": lax.rem(me + step, neurons)}, device_id_type=MESH,
        )

    def token_start(step, carry):
        token_copy(step, me).start()
        return carry

    def token_arrive(step, carry):
        token_copy(step, lax.rem(me + step, neurons)).wait_recv()
        return carry

    def token_leave(step, carry):
        token_copy(step, me).wait_send()
        return carry

    lax.fori_loop(1, neurons, token_start, 0)
    lax.fori_loop(1, neurons, token_arrive, 0)

    def unpack(part, carry):
        arrived = slabs[pl.ds(part * 8, 8), 0:slab_rows, :].astype(F32)
        lhs[pl.ds(pl.multiple_of(part * 16, 16), 16), :] = arrived.reshape(16, subs, LANES).reshape(16, width).astype(BF16)
        return carry

    lax.fori_loop(0, neurons // 8, unpack, 0)
    for source in range(neurons):
        bits_s[2 * source:2 * source + 2, :] = slabs[source, slab_rows:slab_rows + 16, :].astype(F32)[0:2, :]
    active = jnp.dot(bits_s[...].astype(BF16), holds, preferred_element_type=F32)
    for slot in range(slots):
        act[:, slot * BLK:(slot + 1) * BLK] = jnp.broadcast_to(active[:, slot:slot + 1], (rows, BLK))

    def hidden_chunk(index, carry):
        here = pl.ds(pl.multiple_of(index * chunk, chunk), chunk)
        weight_copy(gate_hbm, gate_v, gate_sem, index).wait()
        weight_copy(up_hbm, up_v, up_sem, index).wait()
        contract = (((1,), (1,)), ((), ()))
        gate_pre = lax.dot_general(lhs[...], gate_v[here, :], contract, preferred_element_type=F32)
        up_pre = lax.dot_general(lhs[...], up_v[here, :], contract, preferred_element_type=F32)
        product = jnp.maximum(gate_pre, 0.0) * jnp.maximum(up_pre, 0.0)
        hid[:, here] = (product * act[:, here]).astype(BF16)
        return carry

    lax.fori_loop(0, chunks, hidden_chunk, 0)
    lax.fori_loop(1, neurons, token_leave, 0)

    def out_copy(index, step, row, slot):
        return pltpu.make_async_remote_copy(
            src_ref=snd.at[index, row], dst_ref=rcv.at[index, slot],
            send_sem=out_send.at[index, step], recv_sem=out_recv.at[index, slot],
            device_id={"neuron": lax.rem(me + step, neurons)}, device_id_type=MESH,
        )

    def down_unit(index, carry):
        down_copy(index).wait()
        acc[...] = jnp.dot(hid[...], down_v[index], preferred_element_type=F32)

        def pack(part, inner):
            partial = acc[pl.ds(pl.multiple_of(part * 16, 16), 16), :]
            packed = partial.reshape(16, usubs, LANES).reshape(8, 2 * usubs, LANES)
            snd[index, pl.ds(part * 8, 8)] = packed.astype(BF16)
            return inner

        lax.fori_loop(0, neurons // 8, pack, 0)
        rcv[index, me] = snd[index, me]

        def send(step, inner):
            out_copy(index, step, lax.rem(me + step, neurons), me).start()
            return inner

        lax.fori_loop(1, neurons, send, 0)
        return carry

    lax.fori_loop(0, UNITS, down_unit, 0)

    def fin_copy(index):
        return pltpu.make_async_remote_copy(
            src_ref=rows_own.at[index], dst_ref=rows_other.at[index],
            send_sem=fin_send.at[index], recv_sem=fin_recv.at[index],
            device_id={"expert": other}, device_id_type=MESH,
        )

    upper = lax.broadcasted_iota(jnp.int32, (2 * usubs, LANES), 0) < usubs
    scale_rows = jnp.where(upper, scales[0], scales[1])

    def collect(index, carry):
        def arrive(step, inner):
            source = lax.rem(me + step, neurons)
            out_copy(index, step, source, source).wait_recv()
            return inner

        lax.fori_loop(1, neurons, arrive, 0)
        summed = jnp.sum(rcv[index].astype(F32), axis=0)
        rows_own[index] = summed * scale_rows
        fin_copy(index).start()
        return carry

    lax.fori_loop(0, UNITS, collect, 0)

    offset = (expert * per_dev).astype(F32)
    for index in range(UNITS):
        fin_copy(index).wait_recv()
        mine, others = rows_own[index], rows_other[index]
        tokens_out = []
        for token in range(per_dev):
            place = offset + float(token)
            value = jnp.zeros((usubs, LANES), F32)
            for source, pick_pair in ((mine, picks), (others, picks_other)):
                for row in range(2):
                    gain = (pick_pair[row] == place).astype(F32)
                    value = value + gain * source[row * usubs:(row + 1) * usubs, :]
            tokens_out.append(value[None])
        stacked = jnp.concatenate(tokens_out, axis=0).reshape(per_dev, unit)
        out_ref[:, index * unit:(index + 1) * unit] = stacked.astype(BF16)

    for index in range(UNITS):
        fin_copy(index).wait_send()

    def drain(index, carry):
        def leave(step, inner):
            out_copy(index, step, lax.rem(me + step, neurons), me).wait_send()
            return inner

        return lax.fori_loop(1, neurons, leave, carry)

    lax.fori_loop(0, UNITS, drain, 0)


def local(tokens, routes, route_weights, block_masks, block_list, gate_rows, up_rows, down_rows):
    neurons = lax.axis_size("neuron")
    per_dev, width = tokens.shape
    held = gate_rows.shape[1]
    slots = held // BLK
    chunk_slots = max(size for size in (1, 2, 3) if slots % size == 0)
    chunks = slots // chunk_slots
    rows = 2 * neurons
    subs = width // LANES
    unit = width // UNITS
    usubs = unit // LANES
    vmem = pl.BlockSpec(memory_space=pltpu.VMEM)
    hbm = pl.BlockSpec(memory_space=pl.ANY)
    dma = pltpu.SemaphoreType.DMA
    return pl.pallas_call(
        functools.partial(kernel, neurons, chunk_slots),
        out_shape=jax.ShapeDtypeStruct((per_dev, width), BF16),
        in_specs=[vmem] * 5 + [hbm] * 3,
        out_specs=vmem,
        scratch_shapes=[
            pltpu.VMEM((held, width), BF16),
            pltpu.VMEM((held, width), BF16),
            pltpu.VMEM((UNITS, held, unit), BF16),
            pltpu.VMEM((2, per_dev, subs, LANES), BF16),
            pltpu.VMEM((2,) + routes.shape, jnp.int32),
            pltpu.VMEM((2,) + route_weights.shape, jnp.int32),
            pltpu.VMEM((2,) + block_masks.shape, jnp.int32),
            pltpu.VMEM((neurons, 2 * subs + 16, LANES), BF16),
            pltpu.VMEM((rows, width), BF16),
            pltpu.VMEM((rows, LANES), F32),
            pltpu.VMEM((rows, held), F32),
            pltpu.VMEM((rows, held), BF16),
            pltpu.VMEM((rows, unit), F32),
            pltpu.VMEM((UNITS, neurons, 2 * usubs, LANES), BF16),
            pltpu.VMEM((UNITS, neurons, 2 * usubs, LANES), BF16),
            pltpu.VMEM((UNITS, 2 * usubs, LANES), F32),
            pltpu.VMEM((UNITS, 2 * usubs, LANES), F32),
            dma((chunks,)),
            dma((chunks,)),
            dma((UNITS,)),
            dma((4,)),
            dma((4,)),
            dma((neurons,)),
            dma((neurons,)),
            dma((UNITS, neurons)),
            dma((UNITS, neurons)),
            dma((UNITS,)),
            dma((UNITS,)),
        ],
        compiler_params=pltpu.CompilerParams(
            collective_id=0, has_side_effects=True, vmem_limit_bytes=58 * 1024 * 1024
        ),
    )(tokens, routes, route_weights, block_masks, block_list, gate_rows, up_rows, down_rows)


def solution(mesh):
    placed = (
        P(("groups", "neuron", "expert"), None),
        P(("groups", "neuron", "expert"), None),
        P(("groups", "neuron", "expert"), None),
        P(("groups", "neuron", "expert"), None, None),
        P(("groups", "expert"), None),
        P(("groups", "expert"), "neuron", None),
        P(("groups", "expert"), "neuron", None),
        P(("groups", "expert"), "neuron", None),
    )
    return jax.shard_map(
        local,
        mesh=mesh,
        in_specs=placed,
        out_specs=P(("groups", "neuron", "expert"), None),
        check_vma=False,
    )
```

time: 198 us -> 36.9 us (0.19)
  waiting for transfers between devices: 85.2 us -> 0 us
  blocking collectives: 65 us -> 0 us
  Pallas kernels: 0 us -> 32.6 us
  matrix products: 28.6 us -> 0 us
  local copies, waits for them, and re-layouts: 9.47 us -> 4.04 us
  starting transfers between devices: 4.86 us -> 0 us
  other arithmetic: 3.55 us -> 0 us
    all_to_all x1 -> x0, waiting for transfers between devices: 85.2 us -> none  [local(): lax.all_to_all(block_outputs(lax.all_to_all(outgoing, 'neuron', split_axi...]
    all_to_all x1 -> x0, blocking collectives: 53 us -> none  [local(): lax.all_to_all(outgoing, 'neuron', split_axis=0, concat_axis=0, tiled=True)]
    pallas_call x0 -> x1, Pallas kernels: none -> 32.6 us  [local(): pl.pallas_call(functools.partial(kernel, neurons, chunk_slots), out_shape...]
    dot_general x6 -> x0, matrix products: 28.6 us -> none  [the longest x1 7.74 us: block_outputs(): jnp.einsum('nskd,sud->nsku', arrived, gate_local, preferred_element_type=...]
    all_gather x4 -> x0, blocking collectives: 8.1 us -> none  [the longest x1 2.12 us: local(): lax.all_gather(routes, 'expert', axis=0, tiled=True)]
    transpose x1 -> x0, local copies, waits for them, and re-layouts: 4.93 us -> none  [block_outputs(): jnp.einsum('nsku,sud->nskd', hidden, down_local, preferred_element_type=j...]
    all_to_all x1 -> x0, starting transfers between devices: 4.86 us -> none  [local(): lax.all_to_all(block_outputs(lax.all_to_all(outgoing, 'neuron', split_axi...]
    unnamed x1 -> x0, blocking collectives: 3.85 us -> none
  transfers between devices with their start and end apart: 1 -> 0, of which waited for: 1 -> 0; matrix products, arithmetic and copies ran while one was open for 0% -> 0% of each run, Pallas kernels for 0% -> 0%
where the time goes in v1:
time: 36.9 us; the launch traced here: 36.6 us
  Pallas kernels  32.6 us (88%)
  local copies, waits for them, and re-layouts  4.04 us (11%)
    pallas_call x1, Pallas kernels, local(): pl.pallas_call(functools.partial(kernel, neurons, chunk_slots), out_shape...  32.6 us
    unnamed x3, local copies, waits for them, and re-layouts  4.04 us

profile of v1, /device:TPU:0, one launch (start us, length us, event | category | flops | bytes accessed | tf_op | source)
XLA Modules:
  0.0 36.6 jit_solution(1943806062525785125)
XLA Ops:
  0.0 1.3 %copy.9.routes_in = s32[4,2]{1,0:T(4,128)} copy(s32[4,2]{0,1:T(2,128)} %param.9) | data formatting | bytes 64 | tf_op args[1]
  1.3 1.3 %copy.10.weights_in = s32[4,2]{1,0:T(4,128)} copy(s32[4,2]{0,1:T(2,128)} %param.10) | data formatting | bytes 64 | tf_op args[2]
  2.7 32.6 %shard_map.82 = bf16[4,4096]{1,0:T(4,128)(2,1)} custom-call(bf16[4,4096]{1,0:T(4,128)(2,1)} %tok_in.1, s32[4,2]{1,0:T(4,128)} %copy.9.routes_in, s32[4,2]{1,0:T(4,128)} %copy.10.weights_in, s32[4,2,4]{2,1,0:T(2,128)} %masks_in.1, s32[1,120]{1,0:T(1,128)} %list_in.1, bf16[1,1920,4096]{2,1,0:T(8,128)(2,1)} %gate_hbm.1, bf16[1,1920,4096]{2,1,0:T(8,128)(2,1)} %up_hbm.1, ...), custom_call_target="tpu_custom_call" | custom-call | tf_op jit(solution)/shard_map/pallas_call | solution.py:291
  35.2 1.4 %copy.12 = bf16[4,4096]{1,0:T(4,128)(2,1)} copy(bf16[4,4096]{1,0:T(4,128)(2,1)} %shard_map.82) | data formatting | bytes 65536

commit v2 on v1

v2 whole, which is shorter than its diff:
```python
import functools

import jax
import jax.numpy as jnp
from jax import lax
from jax.experimental import pallas as pl
from jax.experimental.pallas import tpu as pltpu
from jax.sharding import PartitionSpec as P

BLK = 128
LANES = 128
UNITS = 4
PARTS = 2
F32 = jnp.float32
BF16 = jnp.bfloat16
MESH = pl.DeviceIdType.MESH


def total(value, axis):
    return jnp.sum(value, axis=axis, keepdims=True)


def picks_of(expert, routes, places):
    low, high = None, None
    for half in range(2):
        named = jnp.max((routes[half] == expert).astype(F32), axis=0, keepdims=True)
        least = jnp.min(jnp.where(named > 0.5, places[half], 1e6), axis=1, keepdims=True)
        most = jnp.max(jnp.where(named > 0.5, places[half], -1.0), axis=1, keepdims=True)
        low = least if low is None else jnp.minimum(low, least)
        high = most if high is None else jnp.maximum(high, most)
    return low, high


def kernel(
    neurons, group_slots,
    tok_in, routes_in, weights_in, masks_in, list_in, gate_hbm, up_hbm, down_hbm,
    out_ref,
    both_v, down_v, tok_v, list_v, pair_tok, pair_routes, pair_weights, pair_masks, slabs, slab_bits, lhs, bits_s,
    act, pre, hid, acc, snd, rcv, rows_own, rows_other,
    both_sem, down_sem, in_sem, pair_send, pair_recv, tok_send, tok_recv,
    out_send, out_recv, fin_send, fin_recv,
):
    me = lax.axis_index("neuron")
    expert = lax.axis_index("expert")
    other = 1 - expert
    per_dev, width = tok_in.shape
    subs = width // LANES
    part_width = width // PARTS
    part_subs = subs // PARTS
    unit = width // UNITS
    usubs = unit // LANES
    slots = both_v.shape[1]
    rows = 2 * neurons
    groups = slots // group_slots
    few = neurons <= 8

    barrier = pltpu.get_barrier_semaphore()

    def greet(step, carry):
        pl.semaphore_signal(
            barrier, inc=1, device_id={"neuron": lax.rem(me + step, neurons)}, device_id_type=MESH
        )
        return carry

    pl.semaphore_signal(barrier, inc=1, device_id={"expert": other}, device_id_type=MESH)
    lax.fori_loop(1, neurons, greet, 0, unroll=few)

    def small_copies():
        pairs = (
            (tok_in, tok_v), (routes_in, pair_routes.at[expert]), (weights_in, pair_weights.at[expert]),
            (masks_in, pair_masks.at[expert]), (list_in, list_v),
        )
        return [pltpu.make_async_copy(src, dst, in_sem.at[at]) for at, (src, dst) in enumerate(pairs)]

    for copy in small_copies():
        copy.start()

    def both_copies(part, slot):
        columns = pl.ds(part * part_width, part_width)
        here = pl.ds(pl.multiple_of(slot * BLK, BLK), BLK)
        return [
            pltpu.make_async_copy(
                hbm.at[0, here, columns], both_v.at[part, slot, pl.ds(side * BLK, BLK), :],
                both_sem.at[part, slot, side],
            )
            for side, hbm in enumerate((gate_hbm, up_hbm))
        ]

    def down_copy(index):
        return pltpu.make_async_copy(
            down_hbm.at[0, :, pl.ds(index * unit, unit)], down_v.at[index], down_sem.at[index]
        )

    for part in range(PARTS):
        def begin(slot, carry, part=part):
            for copy in both_copies(part, slot):
                copy.start()
            return carry

        lax.fori_loop(0, slots, begin, 0)
    for index in range(UNITS):
        down_copy(index).start()

    for copy in small_copies():
        copy.wait()
    pair_tok[expert] = tok_v[...].astype(F32).reshape(per_dev, subs, LANES).astype(BF16)

    pl.semaphore_wait(barrier, neurons)

    def pair_copy(buffer, index):
        return pltpu.make_async_remote_copy(
            src_ref=buffer.at[expert], dst_ref=buffer.at[expert],
            send_sem=pair_send.at[index], recv_sem=pair_recv.at[index],
            device_id={"expert": other}, device_id_type=MESH,
        )

    pair_buffers = (pair_tok, pair_routes, pair_weights, pair_masks)
    for index, buffer in enumerate(pair_buffers):
        pair_copy(buffer, index).start()

    listed = list_v[...]
    slot_count = listed.shape[1]
    block_id = lax.broadcasted_iota(jnp.int32, (LANES, slot_count), 0)
    slot_id = lax.broadcasted_iota(jnp.int32, (LANES, slot_count), 1).astype(F32)
    first_slot = jnp.min(jnp.where(listed == block_id, slot_id, 1e6), axis=1, keepdims=True)
    own_slot = (lax.broadcasted_iota(jnp.int32, (LANES, LANES), 1) + me * slots).astype(F32)
    slot_lane = lax.broadcasted_iota(jnp.int32, (LANES, LANES), 1)
    holds = ((own_slot == first_slot) & (slot_lane < slots)).astype(F32).astype(BF16)

    for index, buffer in enumerate(pair_buffers):
        pair_copy(buffer, index).wait()

    routes = [pair_routes[half] for half in range(2)]
    places = [
        lax.broadcasted_iota(jnp.int32, (1, per_dev), 1).astype(F32) + float(half * per_dev) for half in range(2)
    ]
    picks = picks_of(expert, routes, places)
    picks_other = picks_of(other, routes, places)

    def token_copy(part, step, source):
        buffer = slabs.at[part, source] if part < PARTS else slab_bits.at[source]
        return pltpu.make_async_remote_copy(
            src_ref=buffer, dst_ref=buffer,
            send_sem=tok_send.at[part, step], recv_sem=tok_recv.at[part, source],
            device_id={"neuron": lax.rem(me + step, neurons)}, device_id_type=MESH,
        )

    def token_start(part):
        def start(step, carry):
            token_copy(part, step, me).start()
            return carry

        lax.fori_loop(1, neurons, start, 0, unroll=few)

    def token_arrive(part):
        def arrive(step, carry):
            token_copy(part, step, lax.rem(me + step, neurons)).wait_recv()
            return carry

        lax.fori_loop(1, neurons, arrive, 0, unroll=few)

    gains = [[(pick == float(token)).astype(F32) for token in range(2 * per_dev)] for pick in picks]
    for part in range(PARTS):
        here = slice(part * part_subs, (part + 1) * part_subs)
        for row in range(2):
            chosen = jnp.zeros((part_subs, LANES), F32)
            for token in range(2 * per_dev):
                chosen = chosen + gains[row][token] * pair_tok[token // per_dev, token % per_dev, here, :].astype(F32)
            slabs[part, me, row * part_subs:(row + 1) * part_subs, :] = chosen.astype(BF16)
        token_start(part)

    lane = lax.broadcasted_iota(jnp.int32, (1, LANES), 1)
    word_of = sum((lane >= 30 * word).astype(jnp.int32) for word in (1, 2, 3))
    shift = jnp.minimum(lane - 30 * word_of, 30)
    scales, bit_rows = [], []
    for row, pick in enumerate(picks):
        scale, words = None, None
        for half in range(2):
            is_it = (routes[half] == expert) & (places[half] == pick)
            weight = total(total(jnp.where(is_it, pair_weights[half].astype(F32), 0.0), 0), 1)
            scale = weight if scale is None else scale + weight
            for token in range(per_dev):
                named = (routes[half][:, token:token + 1] == expert) & (gains[row][half * per_dev + token] > 0.5)
                word = jnp.where(named, pair_masks[half, token], 0)
                words = word if words is None else words + word
        words = total(words, 0)
        scales.append(scale / 65536.0)
        spread = jnp.where(
            word_of == 0, words[:, 0:1],
            jnp.where(word_of == 1, words[:, 1:2], jnp.where(word_of == 2, words[:, 2:3], words[:, 3:4])),
        )
        bit_rows.append(jnp.bitwise_and(jnp.right_shift(spread, shift), 1).astype(F32))
    line = lax.broadcasted_iota(jnp.int32, (16, LANES), 0)
    slab_bits[me] = jnp.where(line == 0, bit_rows[0], jnp.where(line == 1, bit_rows[1], 0.0)).astype(BF16)
    token_start(PARTS)

    def unpack(part):
        def piece(at, carry):
            arrived = slabs[part, pl.ds(at * 8, 8)].astype(F32)
            lhs[part, pl.ds(pl.multiple_of(at * 16, 16), 16), :] = (
                arrived.reshape(16, part_subs, LANES).reshape(16, part_width).astype(BF16)
            )
            return carry

        lax.fori_loop(0, neurons // 8, piece, 0)

    contract = (((1,), (1,)), ((), ()))
    for part in range(PARTS):
        token_arrive(part)
        unpack(part)
        last = part == PARTS - 1
        if last:
            token_arrive(PARTS)
            for source in range(neurons):
                bits_s[2 * source:2 * source + 2, :] = slab_bits[source].astype(F32)[0:2, :]
            active = jnp.dot(bits_s[...].astype(BF16), holds, preferred_element_type=F32)
            for slot in range(slots):
                act[slot] = jnp.broadcast_to(active[:, slot:slot + 1], (rows, BLK))

        def multiply(group, carry, part=part, last=last):
            for inner in range(group_slots):
                for copy in both_copies(part, group * group_slots + inner):
                    copy.wait()
            for inner in range(group_slots):
                slot = group * group_slots + inner
                value = lax.dot_general(lhs[part], both_v[part, slot], contract, preferred_element_type=F32)
                if part > 0:
                    value = value + pre[slot]
                if last:
                    product = jnp.maximum(value[:, :BLK], 0.0) * jnp.maximum(value[:, BLK:], 0.0)
                    hid[:, pl.ds(pl.multiple_of(slot * BLK, BLK), BLK)] = (product * act[slot]).astype(BF16)
                else:
                    pre[slot] = value
            return carry

        lax.fori_loop(0, groups, multiply, 0)

    def out_copy(index, step, row, slot):
        return pltpu.make_async_remote_copy(
            src_ref=snd.at[index, row], dst_ref=rcv.at[index, slot],
            send_sem=out_send.at[index, step], recv_sem=out_recv.at[index, slot],
            device_id={"neuron": lax.rem(me + step, neurons)}, device_id_type=MESH,
        )

    def down_unit(index, carry):
        down_copy(index).wait()
        acc[...] = jnp.dot(hid[...], down_v[index], preferred_element_type=F32)

        def pack(part, inner):
            partial = acc[pl.ds(pl.multiple_of(part * 16, 16), 16), :]
            packed = partial.reshape(16, usubs, LANES).reshape(8, 2 * usubs, LANES)
            snd[index, pl.ds(part * 8, 8)] = packed.astype(BF16)
            return inner

        lax.fori_loop(0, neurons // 8, pack, 0)
        rcv[index, me] = snd[index, me]

        def send(step, inner):
            out_copy(index, step, lax.rem(me + step, neurons), me).start()
            return inner

        lax.fori_loop(1, neurons, send, 0, unroll=few)
        return carry

    lax.fori_loop(0, UNITS, down_unit, 0)

    def fin_copy(index):
        return pltpu.make_async_remote_copy(
            src_ref=rows_own.at[index], dst_ref=rows_other.at[index],
            send_sem=fin_send.at[index], recv_sem=fin_recv.at[index],
            device_id={"expert": other}, device_id_type=MESH,
        )

    upper = lax.broadcasted_iota(jnp.int32, (2 * usubs, LANES), 0) < usubs
    scale_rows = jnp.where(upper, scales[0], scales[1])

    def collect(index, carry):
        def arrive(step, inner):
            source = lax.rem(me + step, neurons)
            out_copy(index, step, source, source).wait_recv()
            return inner

        lax.fori_loop(1, neurons, arrive, 0, unroll=few)
        summed = jnp.sum(rcv[index].astype(F32), axis=0)
        rows_own[index] = summed * scale_rows
        fin_copy(index).start()
        return carry

    lax.fori_loop(0, UNITS, collect, 0)

    offset = (expert * per_dev).astype(F32)
    for index in range(UNITS):
        fin_copy(index).wait_recv()
        mine, others = rows_own[index], rows_other[index]
        tokens_out = []
        for token in range(per_dev):
            place = offset + float(token)
            value = jnp.zeros((usubs, LANES), F32)
            for source, pick_pair in ((mine, picks), (others, picks_other)):
                for row in range(2):
                    gain = (pick_pair[row] == place).astype(F32)
                    value = value + gain * source[row * usubs:(row + 1) * usubs, :]
            tokens_out.append(value[None])
        stacked = jnp.concatenate(tokens_out, axis=0).reshape(per_dev, unit)
        out_ref[:, index * unit:(index + 1) * unit] = stacked.astype(BF16)

    for index in range(UNITS):
        fin_copy(index).wait_send()

    def drain(index, carry):
        def leave(step, inner):
            out_copy(index, step, lax.rem(me + step, neurons), me).wait_send()
            return inner

        return lax.fori_loop(1, neurons, leave, carry, unroll=few)

    lax.fori_loop(0, UNITS, drain, 0)
    for part in range(PARTS + 1):
        def leave_token(step, carry, part=part):
            token_copy(part, step, me).wait_send()
            return carry

        lax.fori_loop(1, neurons, leave_token, 0, unroll=few)


def local(tokens, routes, route_weights, block_masks, block_list, gate_rows, up_rows, down_rows):
    routes, route_weights = routes.T, route_weights.T
    neurons = lax.axis_size("neuron")
    per_dev, width = tokens.shape
    held = gate_rows.shape[1]
    slots = held // BLK
    group_slots = max(size for size in (1, 3, 5) if slots % size == 0)
    rows = 2 * neurons
    subs = width // LANES
    unit = width // UNITS
    usubs = unit // LANES
    part_width = width // PARTS
    vmem = pl.BlockSpec(memory_space=pltpu.VMEM)
    hbm = pl.BlockSpec(memory_space=pl.ANY)
    dma = pltpu.SemaphoreType.DMA
    return pl.pallas_call(
        functools.partial(kernel, neurons, group_slots),
        out_shape=jax.ShapeDtypeStruct((per_dev, width), BF16),
        in_specs=[hbm] * 8,
        out_specs=vmem,
        scratch_shapes=[
            pltpu.VMEM((PARTS, slots, 2 * BLK, part_width), BF16),
            pltpu.VMEM((UNITS, held, unit), BF16),
            pltpu.VMEM((per_dev, width), BF16),
            pltpu.VMEM(block_list.shape, jnp.int32),
            pltpu.VMEM((2, per_dev, subs, LANES), BF16),
            pltpu.VMEM((2,) + routes.shape, jnp.int32),
            pltpu.VMEM((2,) + route_weights.shape, jnp.int32),
            pltpu.VMEM((2,) + block_masks.shape, jnp.int32),
            pltpu.VMEM((PARTS, neurons, 2 * subs // PARTS, LANES), BF16),
            pltpu.VMEM((neurons, 16, LANES), BF16),
            pltpu.VMEM((PARTS, rows, part_width), BF16),
            pltpu.VMEM((rows, LANES), F32),
            pltpu.VMEM((slots, rows, BLK), F32),
            pltpu.VMEM((slots, rows, 2 * BLK), F32),
            pltpu.VMEM((rows, held), BF16),
            pltpu.VMEM((rows, unit), F32),
            pltpu.VMEM((UNITS, neurons, 2 * usubs, LANES), BF16),
            pltpu.VMEM((UNITS, neurons, 2 * usubs, LANES), BF16),
            pltpu.VMEM((UNITS, 2 * usubs, LANES), F32),
            pltpu.VMEM((UNITS, 2 * usubs, LANES), F32),
            dma((PARTS, slots, 2)),
            dma((UNITS,)),
            dma((5,)),
            dma((4,)),
            dma((4,)),
            dma((PARTS + 1, neurons)),
            dma((PARTS + 1, neurons)),
            dma((UNITS, neurons)),
            dma((UNITS, neurons)),
            dma((UNITS,)),
            dma((UNITS,)),
        ],
        compiler_params=pltpu.CompilerParams(
            collective_id=0, has_side_effects=True, vmem_limit_bytes=58 * 1024 * 1024
        ),
    )(tokens, routes, route_weights, block_masks, block_list, gate_rows, up_rows, down_rows)


def solution(mesh):
    placed = (
        P(("groups", "neuron", "expert"), None),
        P(("groups", "neuron", "expert"), None),
        P(("groups", "neuron", "expert"), None),
        P(("groups", "neuron", "expert"), None, None),
        P(("groups", "expert"), None),
        P(("groups", "expert"), "neuron", None),
        P(("groups", "expert"), "neuron", None),
        P(("groups", "expert"), "neuron", None),
    )
    return jax.shard_map(
        local,
        mesh=mesh,
        in_specs=placed,
        out_specs=P(("groups", "neuron", "expert"), None),
        check_vma=False,
    )
```

time: 36.9 us -> 32.7 us (0.89)
  local copies, waits for them, and re-layouts: 4.04 us -> 1.39 us
  Pallas kernels: 32.6 us -> 31.1 us
    unnamed x3 -> x1, local copies, waits for them, and re-layouts: 4.04 us -> 1.39 us
    pallas_call x1, Pallas kernels: 32.6 us -> 31.1 us  [local(): pl.pallas_call(functools.partial(kernel, neurons, group_slots), out_shape...]
where the time goes in v2:
time: 32.7 us; the launch traced here: 32.5 us
  Pallas kernels  31.1 us (95%)
  local copies, waits for them, and re-layouts  1.39 us (4%)
    pallas_call x1, Pallas kernels, local(): pl.pallas_call(functools.partial(kernel, neurons, group_slots), out_shape...  31.1 us
    unnamed x1, local copies, waits for them, and re-layouts  1.39 us

profile of v2, /device:TPU:0, one launch (start us, length us, event | category | flops | bytes accessed | tf_op | source)
XLA Modules:
  0.0 32.5 jit_solution(5244958277537563882)
XLA Ops:
  0.0 31.1 %shard_map.82 = bf16[4,4096]{1,0:T(4,128)(2,1)} custom-call(bf16[4,4096]{1,0:T(4,128)(2,1)} %tok_in.1, s32[2,4]{1,0:T(2,128)} %bitcast.2, s32[2,4]{1,0:T(2,128)} %bitcast.3, s32[4,2,4]{2,1,0:T(2,128)} %masks_in.1, s32[1,120]{1,0:T(1,128)} %list_in.1, bf16[1,1920,4096]{2,1,0:T(8,128)(2,1)} %gate_hbm.1, bf16[1,1920,4096]{2,1,0:T(8,128)(2,1)} %up_hbm.1, ...), custom_call_target="tpu_custom_call" | custom-call | tf_op jit(solution)/shard_map/pallas_call | solution.py:341
  31.1 1.4 %copy.10 = bf16[4,4096]{1,0:T(4,128)(2,1)} copy(bf16[4,4096]{1,0:T(4,128)(2,1)} %shard_map.82) | data formatting | bytes 65536

commit v3 on v2

--- a/solution.py
+++ b/solution.py
@@ -9,7 +9,7 @@
 
 BLK = 128
 LANES = 128
-UNITS = 4
+UNITS = 2
 PARTS = 2
 F32 = jnp.float32
 BF16 = jnp.bfloat16

time: 32.7 us -> 32 us (0.979)
  Pallas kernels: 31.1 us -> 30.5 us
    pallas_call x1, Pallas kernels: 31.1 us -> 30.5 us  [local(): pl.pallas_call(functools.partial(kernel, neurons, group_slots), out_shape...]
where the time goes in v3:
time: 32 us; the launch traced here: 31.8 us
  Pallas kernels  30.5 us (95%)
  local copies, waits for them, and re-layouts  1.39 us (4%)
    pallas_call x1, Pallas kernels, local(): pl.pallas_call(functools.partial(kernel, neurons, group_slots), out_shape...  30.5 us
    unnamed x1, local copies, waits for them, and re-layouts  1.39 us

profile of v3, /device:TPU:0, one launch (start us, length us, event | category | flops | bytes accessed | tf_op | source)
XLA Modules:
  0.0 31.8 jit_solution(4484103418474798840)
XLA Ops:
  0.0 30.5 %shard_map.82 = bf16[4,4096]{1,0:T(4,128)(2,1)} custom-call(bf16[4,4096]{1,0:T(4,128)(2,1)} %tok_in.1, s32[2,4]{1,0:T(2,128)} %bitcast.2, s32[2,4]{1,0:T(2,128)} %bitcast.3, s32[4,2,4]{2,1,0:T(2,128)} %masks_in.1, s32[1,120]{1,0:T(1,128)} %list_in.1, bf16[1,1920,4096]{2,1,0:T(8,128)(2,1)} %gate_hbm.1, bf16[1,1920,4096]{2,1,0:T(8,128)(2,1)} %up_hbm.1, ...), custom_call_target="tpu_custom_call" | custom-call | tf_op jit(solution)/shard_map/pallas_call | solution.py:341
  30.5 1.4 %copy.10 = bf16[4,4096]{1,0:T(4,128)(2,1)} copy(bf16[4,4096]{1,0:T(4,128)(2,1)} %shard_map.82) | data formatting | bytes 65536

commit v4 on v3

--- a/solution.py
+++ b/solution.py
@@ -11,6 +11,9 @@
 LANES = 128
 UNITS = 2
 PARTS = 2
+TILE = 2 * BLK
+CUT1 = 6
+CUT2 = 8
 F32 = jnp.float32
 BF16 = jnp.bfloat16
 MESH = pl.DeviceIdType.MESH
@@ -76,7 +79,7 @@
         copy.start()
 
     def both_copies(part, slot):
-        columns = pl.ds(part * part_width, part_width)
+        columns = pl.ds(pl.multiple_of(part * part_width, part_width), part_width)
         here = pl.ds(pl.multiple_of(slot * BLK, BLK), BLK)
         return [
             pltpu.make_async_copy(
@@ -105,6 +108,23 @@
         copy.wait()
     pair_tok[expert] = tok_v[...].astype(F32).reshape(per_dev, subs, LANES).astype(BF16)
 
+    def turn(pair, carry):
+        for inner in range(2):
+            piece = 2 * pair + inner
+            part = piece // slots
+            slot = piece - part * slots
+            for copy in both_copies(part, slot):
+                copy.wait()
+            for tile in range(part_width // TILE):
+                here = slice(tile * TILE, (tile + 1) * TILE)
+                both_v[part, slot, :, here] = both_v[part, slot, :, here].T
+        return carry
+
+    turned = [groups * group_slots, (groups // 3) * group_slots]
+    if sum(turned) % 2:
+        turned = [0, 0]
+    pairs = sum(turned) // 2
+    lax.fori_loop(0, pairs * CUT1 // 10, turn, 0)
     pl.semaphore_wait(barrier, neurons)
 
     def pair_copy(buffer, index):
@@ -127,6 +147,7 @@
     slot_lane = lax.broadcasted_iota(jnp.int32, (LANES, LANES), 1)
     holds = ((own_slot == first_slot) & (slot_lane < slots)).astype(F32).astype(BF16)
 
+    lax.fori_loop(pairs * CUT1 // 10, pairs * CUT2 // 10, turn, 0)
     for index, buffer in enumerate(pair_buffers):
         pair_copy(buffer, index).wait()
 
@@ -204,7 +225,7 @@
 
         lax.fori_loop(0, neurons // 8, piece, 0)
 
-    contract = (((1,), (1,)), ((), ()))
+    lax.fori_loop(pairs * CUT2 // 10, pairs, turn, 0)
     for part in range(PARTS):
         token_arrive(part)
         unpack(part)
@@ -217,15 +238,22 @@
             for slot in range(slots):
                 act[slot] = jnp.broadcast_to(active[:, slot:slot + 1], (rows, BLK))
 
-        def multiply(group, carry, part=part, last=last):
-            for inner in range(group_slots):
-                for copy in both_copies(part, group * group_slots + inner):
-                    copy.wait()
+        def multiply(group, carry, part, last, square):
+            if not square:
+                for inner in range(group_slots):
+                    for copy in both_copies(part, group * group_slots + inner):
+                        copy.wait()
             for inner in range(group_slots):
                 slot = group * group_slots + inner
-                value = lax.dot_general(lhs[part], both_v[part, slot], contract, preferred_element_type=F32)
-                if part > 0:
-                    value = value + pre[slot]
+                value = pre[slot] if part > 0 else jnp.zeros((rows, 2 * BLK), F32)
+                if not square:
+                    contract = (((1,), (1,)), ((), ()))
+                    value = value + lax.dot_general(
+                        lhs[part], both_v[part, slot], contract, preferred_element_type=F32
+                    )
+                for tile in range(part_width // TILE if square else 0):
+                    here = slice(tile * TILE, (tile + 1) * TILE)
+                    value = value + jnp.dot(lhs[part, :, here], both_v[part, slot, :, here], preferred_element_type=F32)
                 if last:
                     product = jnp.maximum(value[:, :BLK], 0.0) * jnp.maximum(value[:, BLK:], 0.0)
                     hid[:, pl.ds(pl.multiple_of(slot * BLK, BLK), BLK)] = (product * act[slot]).astype(BF16)
@@ -233,7 +261,11 @@
                     pre[slot] = value
             return carry
 
-        lax.fori_loop(0, groups, multiply, 0)
+        ready = turned[part] // group_slots
+        if ready:
+            lax.fori_loop(0, ready, functools.partial(multiply, part=part, last=last, square=True), 0)
+        if ready < groups:
+            lax.fori_loop(ready, groups, functools.partial(multiply, part=part, last=last, square=False), 0)
 
     def out_copy(index, step, row, slot):
         return pltpu.make_async_remote_copy(

time: 32 us -> 31.6 us (0.988)
  Pallas kernels: 30.5 us -> 30 us
    pallas_call x1, Pallas kernels: 30.5 us -> 30 us  [local(): pl.pallas_call(functools.partial(kernel, neurons, group_slots), out_shape...]
where the time goes in v4:
time: 31.6 us; the launch traced here: 31.4 us
  Pallas kernels  30 us (95%)
  local copies, waits for them, and re-layouts  1.39 us (4%)
    pallas_call x1, Pallas kernels, local(): pl.pallas_call(functools.partial(kernel, neurons, group_slots), out_shape...  30 us
    unnamed x1, local copies, waits for them, and re-layouts  1.39 us

profile of v4, /device:TPU:0, one launch (start us, length us, event | category | flops | bytes accessed | tf_op | source)
XLA Modules:
  0.0 31.4 jit_solution(5967083563701217690)
XLA Ops:
  0.0 30.0 %shard_map.82 = bf16[4,4096]{1,0:T(4,128)(2,1)} custom-call(bf16[4,4096]{1,0:T(4,128)(2,1)} %tok_in.1, s32[2,4]{1,0:T(2,128)} %bitcast.2, s32[2,4]{1,0:T(2,128)} %bitcast.3, s32[4,2,4]{2,1,0:T(2,128)} %masks_in.1, s32[1,120]{1,0:T(1,128)} %list_in.1, bf16[1,1920,4096]{2,1,0:T(8,128)(2,1)} %gate_hbm.1, bf16[1,1920,4096]{2,1,0:T(8,128)(2,1)} %up_hbm.1, ...), custom_call_target="tpu_custom_call" | custom-call | tf_op jit(solution)/shard_map/pallas_call | solution.py:373
  30.0 1.4 %copy.10 = bf16[4,4096]{1,0:T(4,128)(2,1)} copy(bf16[4,4096]{1,0:T(4,128)(2,1)} %shard_map.82) | data formatting | bytes 65536
